TPU v7x, 32 devices: a whole 2x2x4 slice. The times are simulated.
32 devices in a mesh: groups: 2 (over y), pts: 4 (over z), seg: 4 (over x, core).
Axes of the slice: x: 2, y: 2, z: 4, core: 2. Of those that a mesh axis runs over, the one named last changes fastest.
Arguments:
- field_points: float32 [3, 8192], P(None, ('groups', 'pts', 'seg')), parts along dimension 1, may hold values from -6 to 6
- wake_nodes: float32 [3, 65536], P(None, ('groups', 'seg')), parts along dimension 1, may hold values from -6 to 6
- trail_node: int32 [65536], P(('groups', 'seg')), parts along dimension 0, may hold values from 0 to 8191
- strength: float32 [65536], P(('groups', 'seg')), parts along dimension 0, may hold values from -3 to 3
- core_square: float32 [65536], P(('groups', 'seg')), parts along dimension 0, may hold values from 0.05 to 0.5
- snapshot: int32 [65536], P(('groups', 'seg')), parts along dimension 0, may hold values from 0 to 15
- stored_modes: float32 [512, 8192], P(None, ('groups', 'pts', 'seg')), parts along dimension 1, may hold values from -0.03125 to 0.03125
Outputs:
- coeffs: float32 [1024, 48], P('groups'), parts along dimension 0
- factor: float32 [96, 48], P('groups'), parts along dimension 0
- basis: float32 [48, 8192], P(None, ('groups', 'pts', 'seg')), parts along dimension 1
There are 2 independent parts, one for each index of `groups`. A program takes and returns all parts, laid end to end along the dimension named above; each array names one. Nothing has to cross between parts.
All inputs are finite; a program needn't handle non-finite values.
Results may differ from a plain program's by a relative error of at most 0.0003.
Values sent between devices are 32-bit elements; how exact they have to be, the bound alone decides.
A program may use at most 192 MiB of HBM per device.

v0:
```python
import math

import jax
import jax.numpy as jnp
from jax import lax
from jax.sharding import PartitionSpec as P

SNAPS = 16


HIGH = lax.Precision.HIGHEST
inv_four_pi = 1.0 / (4.0 * math.pi)


def induced_block(points, geometry, labels):
    seg_tail = geometry[0:3]
    seg_head = geometry[3:6]
    near_arm = points[:, :, None] - seg_tail[:, None, :]
    far_arm = points[:, :, None] - seg_head[:, None, :]
    core_sq = geometry[7][None, :]
    near_len = jnp.sqrt(jnp.sum(near_arm * near_arm, axis=0) + core_sq)
    far_len = jnp.sqrt(jnp.sum(far_arm * far_arm, axis=0) + core_sq)
    along_dot = jnp.sum(near_arm * far_arm, axis=0)
    factor = (near_len + far_len) / (near_len * far_len * (near_len * far_len + along_dot))
    curl_dir = (
        jnp.stack(
            [
                near_arm[1] * far_arm[2] - near_arm[2] * far_arm[1],
                near_arm[2] * far_arm[0] - near_arm[0] * far_arm[2],
                near_arm[0] * far_arm[1] - near_arm[1] * far_arm[0],
            ]
        )
        * factor[None]
    )
    levels = jnp.arange(SNAPS, dtype=jnp.float32)
    weights = (labels[:, None] == levels[None, :]).astype(jnp.float32) * (
        geometry[6] * inv_four_pi
    )[:, None]
    induced = jnp.einsum("cpn,ns->csp", curl_dir, weights, precision=HIGH)
    return induced.reshape(3 * SNAPS, points.shape[1])


def induced_all(points, geometry):
    seg_count = geometry.shape[1]
    block_width = math.gcd(seg_count, 2048)
    block_count = seg_count // block_width

    def one_block(block, running):
        piece = lax.dynamic_slice_in_dim(geometry, block * block_width, block_width, 1)
        return running + induced_block(points, piece, piece[8])

    start_val = jnp.zeros((3 * SNAPS, points.shape[1]), jnp.float32)
    return lax.fori_loop(0, block_count, one_block, start_val)


def matmul(left, right):
    return jnp.dot(left, right, precision=HIGH, preferred_element_type=jnp.float32)


def body(field_points, wake_nodes, trail_node, strength, core_square, snapshot, stored_modes):
    seg_ends = wake_nodes[:, trail_node]
    geometry = jnp.concatenate(
        [
            wake_nodes,
            seg_ends,
            strength[None],
            core_square[None],
            snapshot.astype(jnp.float32)[None],
        ],
        axis=0,
    )
    local_count = field_points.shape[1]
    total_points = local_count * lax.axis_size("pts") * lax.axis_size("seg")
    panel = induced_all(field_points, lax.all_gather(geometry, "seg", axis=1, tiled=True))
    coeffs = lax.psum(matmul(stored_modes, panel.T), ("pts", "seg"))
    projected = panel - matmul(coeffs.T, stored_modes)
    gram = lax.psum(matmul(projected, projected.T), ("pts", "seg")) / total_points
    lower = jnp.linalg.cholesky(gram)
    basis = lax.linalg.triangular_solve(lower, projected, left_side=True, lower=True)
    return (coeffs, lower.T, basis)


def solution(mesh):
    return jax.shard_map(
        body,
        mesh=mesh,
        in_specs=(
            P(None, ("groups", "pts", "seg")),
            P(None, ("groups", "seg")),
            P(("groups", "seg")),
            P(("groups", "seg")),
            P(("groups", "seg")),
            P(("groups", "seg")),
            P(None, ("groups", "pts", "seg")),
        ),
        out_specs=(P("groups", None), P("groups", None), P(None, ("groups", "pts", "seg"))),
        check_vma=False,
    )
```

profile of v0, /device:TPU:0, one launch (start us, length us, event | category | flops | bytes accessed | tf_op | source)
XLA Modules:
  0.0 621.8 jit_solution(7920889873345197063)
XLA Ops:
  10.7 29.9 %gather_fusion = f32[8192,3]{1,0:T(8,128)} fusion(f32[3,8192]{0,1:T(8,128)} %copy.25, s32[8192]{0:T(1024)S(1)} %fusion.14), kind=kCustom, calls=%fused_computation | custom fusion | bytes 229376 | tf_op jit(solution)/shard_map/gather | solution.py:61
  45.3 25.4 %all-gather.2.cloned.1.call-done = f32[9,32768]{1,0:T(8,128)} async-done(((f32[9,8192]{1,0:T(8,128)}), f32[9,32768]{1,0:T(8,128)}) %all-gather.2.cloned.1.call-update) | async-done | bytes 1179664 | tf_op jit(solution)/shard_map/all_gather | solution.py:74
  70.7 383.1 %while.14 = (s32[]{:T(128)}, f32[48,256]{1,0:T(8,128)S(1)}, f32[9,32768]{1,0:T(8,128)}, f32[3,256]{1,0:T(4,128)S(1)}, s32[]{:T(128)}, /*index=5*/s32[]{:T(128)},...) while((s32[]{:T(128)}, f32[48,256]{1,0:T(8,128)S(1)}, f32[9,32768]{1,0:T(8,128)}, ...), condition=%wide.region_4.0_spmd.clone, body=%wide.region_0.0_spmd.clone.sunk | while | flops 326199296 | bytes 80112912 | solution.py:53
  71.7 8.3 %multiply_reduce_fusion.4 = (f32[256,2048]{1,0:T(8,128)S(1)}, f32[256,2048]{1,0:T(8,128)}, f32[256,2048]{1,0:T(8,128)}, f32[3,256,2048]{2,1,0:T(8,128)}, f32[3,256,2048]{2,1,0:T(8,128)}) fusion(f32[3,2048]{1,0:T(4,128)S(1)} %get-tuple-element.176, f32[3,256]{1,0:T(4,128)S(1)} %get-tuple-element.216, f32[3,2048]{1,0:T(4,128)S(1)} %get-tuple-element.177), kind=kLoop, calls=%fused_computation.9.clone.1 | loop fusion | flops 11010048 | bytes 18926592 | tf_op jit(solution)/shard_map/while/body/eval_jaxpr/reduce_sum | solution.py:21
  89.3 5.3 fusion.38
  95.6 8.3 %multiply_reduce_fusion.4 = (f32[256,2048]{1,0:T(8,128)S(1)}, f32[256,2048]{1,0:T(8,128)}, f32[256,2048]{1,0:T(8,128)}, f32[3,256,2048]{2,1,0:T(8,128)}, f32[3,256,2048]{2,1,0:T(8,128)}) fusion(f32[3,2048]{1,0:T(4,128)S(1)} %get-tuple-element.176, f32[3,256]{1,0:T(4,128)S(1)} %get-tuple-element.216, f32[3,2048]{1,0:T(4,128)S(1)} %get-tuple-element.177), kind=kLoop, calls=%fused_computation.9.clone.1 | loop fusion | flops 11010048 | bytes 18926592 | tf_op jit(solution)/shard_map/while/body/eval_jaxpr/reduce_sum | solution.py:21
  113.3 5.3 fusion.38
  119.6 8.3 %multiply_reduce_fusion.4 = (f32[256,2048]{1,0:T(8,128)S(1)}, f32[256,2048]{1,0:T(8,128)}, f32[256,2048]{1,0:T(8,128)}, f32[3,256,2048]{2,1,0:T(8,128)}, f32[3,256,2048]{2,1,0:T(8,128)}) fusion(f32[3,2048]{1,0:T(4,128)S(1)} %get-tuple-element.176, f32[3,256]{1,0:T(4,128)S(1)} %get-tuple-element.216, f32[3,2048]{1,0:T(4,128)S(1)} %get-tuple-element.177), kind=kLoop, calls=%fused_computation.9.clone.1 | loop fusion | flops 11010048 | bytes 18926592 | tf_op jit(solution)/shard_map/while/body/eval_jaxpr/reduce_sum | solution.py:21
  137.2 5.3 fusion.38
  143.5 8.3 %multiply_reduce_fusion.4 = (f32[256,2048]{1,0:T(8,128)S(1)}, f32[256,2048]{1,0:T(8,128)}, f32[256,2048]{1,0:T(8,128)}, f32[3,256,2048]{2,1,0:T(8,128)}, f32[3,256,2048]{2,1,0:T(8,128)}) fusion(f32[3,2048]{1,0:T(4,128)S(1)} %get-tuple-element.176, f32[3,256]{1,0:T(4,128)S(1)} %get-tuple-element.216, f32[3,2048]{1,0:T(4,128)S(1)} %get-tuple-element.177), kind=kLoop, calls=%fused_computation.9.clone.1 | loop fusion | flops 11010048 | bytes 18926592 | tf_op jit(solution)/shard_map/while/body/eval_jaxpr/reduce_sum | solution.py:21
  167.5 8.3 %multiply_reduce_fusion.4 = (f32[256,2048]{1,0:T(8,128)S(1)}, f32[256,2048]{1,0:T(8,128)}, f32[256,2048]{1,0:T(8,128)}, f32[3,256,2048]{2,1,0:T(8,128)}, f32[3,256,2048]{2,1,0:T(8,128)}) fusion(f32[3,2048]{1,0:T(4,128)S(1)} %get-tuple-element.176, f32[3,256]{1,0:T(4,128)S(1)} %get-tuple-element.216, f32[3,2048]{1,0:T(4,128)S(1)} %get-tuple-element.177), kind=kLoop, calls=%fused_computation.9.clone.1 | loop fusion | flops 11010048 | bytes 18926592 | tf_op jit(solution)/shard_map/while/body/eval_jaxpr/reduce_sum | solution.py:21
  191.4 8.3 %multiply_reduce_fusion.4 = (f32[256,2048]{1,0:T(8,128)S(1)}, f32[256,2048]{1,0:T(8,128)}, f32[256,2048]{1,0:T(8,128)}, f32[3,256,2048]{2,1,0:T(8,128)}, f32[3,256,2048]{2,1,0:T(8,128)}) fusion(f32[3,2048]{1,0:T(4,128)S(1)} %get-tuple-element.176, f32[3,256]{1,0:T(4,128)S(1)} %get-tuple-element.216, f32[3,2048]{1,0:T(4,128)S(1)} %get-tuple-element.177), kind=kLoop, calls=%fused_computation.9.clone.1 | loop fusion | flops 11010048 | bytes 18926592 | tf_op jit(solution)/shard_map/while/body/eval_jaxpr/reduce_sum | solution.py:21
  215.4 8.3 %multiply_reduce_fusion.4 = (f32[256,2048]{1,0:T(8,128)S(1)}, f32[256,2048]{1,0:T(8,128)}, f32[256,2048]{1,0:T(8,128)}, f32[3,256,2048]{2,1,0:T(8,128)}, f32[3,256,2048]{2,1,0:T(8,128)}) fusion(f32[3,2048]{1,0:T(4,128)S(1)} %get-tuple-element.176, f32[3,256]{1,0:T(4,128)S(1)} %get-tuple-element.216, f32[3,2048]{1,0:T(4,128)S(1)} %get-tuple-element.177), kind=kLoop, calls=%fused_computation.9.clone.1 | loop fusion | flops 11010048 | bytes 18926592 | tf_op jit(solution)/shard_map/while/body/eval_jaxpr/reduce_sum | solution.py:21
  239.3 8.3 %multiply_reduce_fusion.4 = (f32[256,2048]{1,0:T(8,128)S(1)}, f32[256,2048]{1,0:T(8,128)}, f32[256,2048]{1,0:T(8,128)}, f32[3,256,2048]{2,1,0:T(8,128)}, f32[3,256,2048]{2,1,0:T(8,128)}) fusion(f32[3,2048]{1,0:T(4,128)S(1)} %get-tuple-element.176, f32[3,256]{1,0:T(4,128)S(1)} %get-tuple-element.216, f32[3,2048]{1,0:T(4,128)S(1)} %get-tuple-element.177), kind=kLoop, calls=%fused_computation.9.clone.1 | loop fusion | flops 11010048 | bytes 18926592 | tf_op jit(solution)/shard_map/while/body/eval_jaxpr/reduce_sum | solution.py:21
  263.2 8.3 %multiply_reduce_fusion.4 = (f32[256,2048]{1,0:T(8,128)S(1)}, f32[256,2048]{1,0:T(8,128)}, f32[256,2048]{1,0:T(8,128)}, f32[3,256,2048]{2,1,0:T(8,128)}, f32[3,256,2048]{2,1,0:T(8,128)}) fusion(f32[3,2048]{1,0:T(4,128)S(1)} %get-tuple-element.176, f32[3,256]{1,0:T(4,128)S(1)} %get-tuple-element.216, f32[3,2048]{1,0:T(4,128)S(1)} %get-tuple-element.177), kind=kLoop, calls=%fused_computation.9.clone.1 | loop fusion | flops 11010048 | bytes 18926592 | tf_op jit(solution)/shard_map/while/body/eval_jaxpr/reduce_sum | solution.py:21
  287.2 8.3 %multiply_reduce_fusion.4 = (f32[256,2048]{1,0:T(8,128)S(1)}, f32[256,2048]{1,0:T(8,128)}, f32[256,2048]{1,0:T(8,128)}, f32[3,256,2048]{2,1,0:T(8,128)}, f32[3,256,2048]{2,1,0:T(8,128)}) fusion(f32[3,2048]{1,0:T(4,128)S(1)} %get-tuple-element.176, f32[3,256]{1,0:T(4,128)S(1)} %get-tuple-element.216, f32[3,2048]{1,0:T(4,128)S(1)} %get-tuple-element.177), kind=kLoop, calls=%fused_computation.9.clone.1 | loop fusion | flops 11010048 | bytes 18926592 | tf_op jit(solution)/shard_map/while/body/eval_jaxpr/reduce_sum | solution.py:21
  311.1 8.3 %multiply_reduce_fusion.4 = (f32[256,2048]{1,0:T(8,128)S(1)}, f32[256,2048]{1,0:T(8,128)}, f32[256,2048]{1,0:T(8,128)}, f32[3,256,2048]{2,1,0:T(8,128)}, f32[3,256,2048]{2,1,0:T(8,128)}) fusion(f32[3,2048]{1,0:T(4,128)S(1)} %get-tuple-element.176, f32[3,256]{1,0:T(4,128)S(1)} %get-tuple-element.216, f32[3,2048]{1,0:T(4,128)S(1)} %get-tuple-element.177), kind=kLoop, calls=%fused_computation.9.clone.1 | loop fusion | flops 11010048 | bytes 18926592 | tf_op jit(solution)/shard_map/while/body/eval_jaxpr/reduce_sum | solution.py:21
  335.1 8.3 %multiply_reduce_fusion.4 = (f32[256,2048]{1,0:T(8,128)S(1)}, f32[256,2048]{1,0:T(8,128)}, f32[256,2048]{1,0:T(8,128)}, f32[3,256,2048]{2,1,0:T(8,128)}, f32[3,256,2048]{2,1,0:T(8,128)}) fusion(f32[3,2048]{1,0:T(4,128)S(1)} %get-tuple-element.176, f32[3,256]{1,0:T(4,128)S(1)} %get-tuple-element.216, f32[3,2048]{1,0:T(4,128)S(1)} %get-tuple-element.177), kind=kLoop, calls=%fused_computation.9.clone.1 | loop fusion | flops 11010048 | bytes 18926592 | tf_op jit(solution)/shard_map/while/body/eval_jaxpr/reduce_sum | solution.py:21
  359.0 8.3 %multiply_reduce_fusion.4 = (f32[256,2048]{1,0:T(8,128)S(1)}, f32[256,2048]{1,0:T(8,128)}, f32[256,2048]{1,0:T(8,128)}, f32[3,256,2048]{2,1,0:T(8,128)}, f32[3,256,2048]{2,1,0:T(8,128)}) fusion(f32[3,2048]{1,0:T(4,128)S(1)} %get-tuple-element.176, f32[3,256]{1,0:T(4,128)S(1)} %get-tuple-element.216, f32[3,2048]{1,0:T(4,128)S(1)} %get-tuple-element.177), kind=kLoop, calls=%fused_computation.9.clone.1 | loop fusion | flops 11010048 | bytes 18926592 | tf_op jit(solution)/shard_map/while/body/eval_jaxpr/reduce_sum | solution.py:21
  383.0 8.3 %multiply_reduce_fusion.4 = (f32[256,2048]{1,0:T(8,128)S(1)}, f32[256,2048]{1,0:T(8,128)}, f32[256,2048]{1,0:T(8,128)}, f32[3,256,2048]{2,1,0:T(8,128)}, f32[3,256,2048]{2,1,0:T(8,128)}) fusion(f32[3,2048]{1,0:T(4,128)S(1)} %get-tuple-element.176, f32[3,256]{1,0:T(4,128)S(1)} %get-tuple-element.216, f32[3,2048]{1,0:T(4,128)S(1)} %get-tuple-element.177), kind=kLoop, calls=%fused_computation.9.clone.1 | loop fusion | flops 11010048 | bytes 18926592 | tf_op jit(solution)/shard_map/while/body/eval_jaxpr/reduce_sum | solution.py:21
  406.9 8.3 %multiply_reduce_fusion.4 = (f32[256,2048]{1,0:T(8,128)S(1)}, f32[256,2048]{1,0:T(8,128)}, f32[256,2048]{1,0:T(8,128)}, f32[3,256,2048]{2,1,0:T(8,128)}, f32[3,256,2048]{2,1,0:T(8,128)}) fusion(f32[3,2048]{1,0:T(4,128)S(1)} %get-tuple-element.176, f32[3,256]{1,0:T(4,128)S(1)} %get-tuple-element.216, f32[3,2048]{1,0:T(4,128)S(1)} %get-tuple-element.177), kind=kLoop, calls=%fused_computation.9.clone.1 | loop fusion | flops 11010048 | bytes 18926592 | tf_op jit(solution)/shard_map/while/body/eval_jaxpr/reduce_sum | solution.py:21
  430.8 8.3 %multiply_reduce_fusion.4 = (f32[256,2048]{1,0:T(8,128)S(1)}, f32[256,2048]{1,0:T(8,128)}, f32[256,2048]{1,0:T(8,128)}, f32[3,256,2048]{2,1,0:T(8,128)}, f32[3,256,2048]{2,1,0:T(8,128)}) fusion(f32[3,2048]{1,0:T(4,128)S(1)} %get-tuple-element.176, f32[3,256]{1,0:T(4,128)S(1)} %get-tuple-element.216, f32[3,2048]{1,0:T(4,128)S(1)} %get-tuple-element.177), kind=kLoop, calls=%fused_computation.9.clone.1 | loop fusion | flops 11010048 | bytes 18926592 | tf_op jit(solution)/shard_map/while/body/eval_jaxpr/reduce_sum | solution.py:21
  455.0 87.3 %all-reduce.2.cloned.1.call-done = f32[512,48]{0,1:T(8,128)} async-done(((f32[512,48]{0,1:T(8,128)}), f32[512,48]{0,1:T(8,128)}) %all-reduce.2.cloned.1.call-update) | async-done | bytes 98320 | tf_op jit(solution)/shard_map/psum | solution.py:75
  543.8 58.6 %psum.15 = f32[48,48]{0,1:T(8,128)S(1)} all-reduce(f32[48,48]{0,1:T(8,128)S(1)} %fusion.21), channel_id=1, replica_groups=mesh['groups'=2,'pts'=4,'seg'=4] {'pts','seg'}, use_global_device_ids=true, to_apply=%region_6.0 | all-reduce | flops 2304 | bytes 18432 | tf_op jit(solution)/shard_map/psum | solution.py:77
  (163 shorter events, 257.3 us)
Async XLA Ops:
  7.2 446.6 %copy-start = (f32[512,256]{1,0:T(8,128)S(1)}, f32[512,256]{1,0:T(8,128)}, u32[]{:S(2)}) copy-start(f32[512,256]{1,0:T(8,128)} %param.15) | copy-start | bytes 1572868
  7.2 3.5 copy-start.6
  7.2 63.5 %all-gather.2.cloned.1.call-start = ((), (), s32[]{:S(2)}) async-start(), calls=%async_computation | async-start | bytes 2621440 | tf_op jit(solution)/shard_map/all_gather | solution.py:74
  40.6 2.9 copy-start.2
  40.6 2.9 copy-start.4
  40.7 2.9 copy-start.5
  40.7 30.0 %copy-start.3 = (f32[3,256]{1,0:T(4,128)S(1)}, f32[3,256]{1,0:T(4,128)}, u32[]{:S(2)}) copy-start(f32[3,256]{1,0:T(4,128)} %param.9) | copy-start | bytes 9220
  45.3 497.1 %all-reduce.2.cloned.1.call-start = ((), (), s32[]{:S(2)}) async-start(), calls=%async_computation.1 | async-start | bytes 196608 | tf_op jit(solution)/shard_map/psum | solution.py:75
  81.0 4.1 copy-start.1
  104.9 4.1 copy-start.1
  128.9 4.1 copy-start.1
  152.8 4.1 copy-start.1
  176.8 4.1 copy-start.1
  200.7 4.1 copy-start.1
  224.7 4.1 copy-start.1
  248.6 4.1 copy-start.1
  272.5 4.1 copy-start.1
  296.5 4.1 copy-start.1
  320.4 4.1 copy-start.1
  344.4 4.1 copy-start.1
  368.3 4.1 copy-start.1
  392.3 4.1 copy-start.1
  416.2 4.1 copy-start.1
  440.1 4.1 copy-start.1
  (1 other events, 2.9 us)
Sparse Core Ops, SparseCore 0:
  45.4 25.2 all-gather.1
  455.1 87.1 all-reduce.1
where the time goes:
time: 624 us; the launch traced here: 622 us
  other arithmetic  289 us (46%)
  waiting for transfers between devices  113 us (18%)
  matrix products  87.6 us (14%)
  local copies, waits for them, and re-layouts  59 us (9%)
  blocking collectives  58.6 us (9%)
  between operations  14.2 us (2%)
    reduce_sum x16, other arithmetic, induced_block(): near_len = jnp.sqrt(jnp.sum(near_arm * near_arm, axis=0) + core_sq)  133 us
    psum x1, waiting for transfers between devices, body(): coeffs = lax.psum(matmul(stored_modes, panel.T), ('pts', 'seg'))  87.3 us
    dot_general x16, matrix products, induced_block(): induced = jnp.einsum('cpn,ns->csp', curl_dir, weights, precision=HIGH)  84 us
    sub x16, other arithmetic, induced_block(): near_arm[1] * far_arm[2] - near_arm[2] * far_arm[1]  68.4 us
    div x16, other arithmetic, induced_block(): (near_len + far_len) / (near_len * far_len * (near_len * far_len + along_...  61.9 us
    psum x1, blocking collectives, body(): lax.psum(matmul(projected, projected.T), ('pts', 'seg')) / total_points  58.6 us
    gather x2, local copies, waits for them, and re-layouts, body(): seg_ends = wake_nodes[:, trail_node]  32.8 us
    all_gather x1, waiting for transfers between devices, body(): lax.all_gather(geometry, 'seg', axis=1, tiled=True)  25.4 us
  transfers between devices with their start and end apart: 2, of which 2 were waited for; matrix products, arithmetic and copies ran while one was open for 0% of the time, Pallas kernels for 0%

commit v1 on v0

v1 whole, which is shorter than its diff:
```python
import functools
import math

import jax
import jax.numpy as jnp
from jax import lax
from jax.experimental import pallas as pl
from jax.experimental.pallas import tpu as pltpu
from jax.sharding import PartitionSpec as P

SNAPS = 16
HIGH = lax.Precision.HIGHEST
MESH = pl.DeviceIdType.MESH
DEPTH = 32
CHUNK = 256
GROUP = 4
f32 = jnp.float32
bf16 = jnp.bfloat16


def split3(v):
    hi = v.astype(bf16).astype(f32)
    rest = v - hi
    mid = rest.astype(bf16).astype(f32)
    return hi, mid, (rest - mid).astype(bf16).astype(f32)


def left_rows(v):
    hi, mid, lo = split3(v)
    return [hi, hi, mid, hi, lo, mid]


def right_rows(v):
    hi, mid, lo = split3(v)
    return [hi, mid, hi, lo, hi, mid]


def prep_kernel(nodes_ref, trail_ref, strength_ref, core_ref, snap_ref,
                near_ref, far_ref, weight_ref, centre_ref, head_ref):
    segs = nodes_ref.shape[1]
    rows = segs // 128
    nodes = nodes_ref[...]
    centre = jnp.sum(nodes, axis=1, keepdims=True) * (1.0 / segs)
    centre_ref[...] = jnp.broadcast_to(centre, centre_ref.shape)

    tiles = rows // 8
    high = [trail_ref[8 * r:8 * r + 8, :] // 128 for r in range(tiles)]
    low = [trail_ref[8 * r:8 * r + 8, :] % 128 for r in range(tiles)]

    def look(h, found):
        cols = pl.ds(pl.multiple_of(h * 128, 128), 128)
        out = list(found)
        table = [jnp.broadcast_to(nodes_ref[k:k + 1, cols], (8, 128)) for k in range(3)]
        for r in range(tiles):
            here = high[r] == h
            for k in range(3):
                got = jnp.take_along_axis(table[k], low[r], axis=1, mode="promise_in_bounds")
                out[3 * r + k] = jnp.where(here, got, out[3 * r + k])
        return tuple(out)

    found = lax.fori_loop(0, rows, look, tuple(jnp.zeros((8, 128), f32) for _ in range(3 * tiles)))
    for r in range(tiles):
        for k in range(3):
            for i in range(8):
                at = (8 * r + i) * 128
                head_ref[k:k + 1, at:at + 128] = found[3 * r + k][i:i + 1, :]

    width = 1024
    zero = jnp.zeros((1, width), f32)
    levels = lax.broadcasted_iota(jnp.int32, (SNAPS, width), 0)

    def fill(b, carry):
        cols = pl.ds(pl.multiple_of(b * width, 128), width)
        t = [nodes_ref[k:k + 1, cols] - centre[k:k + 1, :] for k in range(3)]
        h = [head_ref[k:k + 1, cols] - centre[k:k + 1, :] for k in range(3)]
        core = core_ref[:, cols]
        d = [t[k] - h[k] for k in range(3)]
        q = 2.0 * core + (d[0] * d[0] + d[1] * d[1] + d[2] * d[2])
        g = 1.0 / q
        for ref, e in ((near_ref, t), (far_ref, h)):
            square = e[0] * e[0] + e[1] * e[1] + e[2] * e[2] + core
            parts = []
            for k in range(3):
                parts += left_rows(-2.0 * g * e[k])
            parts += left_rows(g) + list(split3(g * square))
            parts += [zero] * (DEPTH - len(parts))
            packed = jnp.concatenate(parts, axis=0)
            ref[pl.ds(pl.multiple_of(b * width, 128), width), :] = packed.T.astype(bf16)
        scale = strength_ref[:, cols] * (2.0 / (4.0 * math.pi)) * g * jnp.sqrt(g)
        v = d + [t[1] * h[2] - t[2] * h[1], t[2] * h[0] - t[0] * h[2], t[0] * h[1] - t[1] * h[0]]
        mine = snap_ref[:, cols] == levels
        for k in range(6):
            value = v[k] * scale
            hi = value.astype(bf16).astype(f32)
            lo = value - hi
            at = SNAPS * k
            weight_ref[at:at + SNAPS, cols] = jnp.where(mine, hi, 0.0).astype(bf16)
            weight_ref[6 * SNAPS + at:6 * SNAPS + at + SNAPS, cols] = jnp.where(mine, lo, 0.0).astype(bf16)
        return carry

    lax.fori_loop(0, segs // width, fill, 0)


def main_kernel(pts_size, seg_size, points_ref, near_ref, far_ref, weight_ref, centre_ref, modes_ref,
                coeff_ref, gram_ref, proj_ref,
                peer_points, part_out, part_in, both_acc, low_acc, side, hi_buf, lo_buf,
                coeff_in, gram_in,
                point_send, point_recv, part_send, part_recv, coeff_send, coeff_recv, gram_send, gram_recv):
    group = lax.axis_index("groups")
    pts = lax.axis_index("pts")
    seg = lax.axis_index("seg")
    count = pts_size * seg_size
    bits = count.bit_length() - 1
    flat = pts * seg_size + seg
    segs = near_ref.shape[0]
    local = points_ref.shape[1]

    def seg_peer(d):
        return (group, pts, lax.rem(seg + d, seg_size))

    def bit_peer(k):
        bit = 1 << k
        other = flat + (1 - 2 * ((flat // bit) % 2)) * bit
        return (group, other // seg_size, other % seg_size)

    peers = [seg_peer(d) for d in range(1, seg_size)]
    peers += [bit_peer(k) for k in range(bits)]
    barrier = pltpu.get_barrier_semaphore()
    for peer in peers:
        pl.semaphore_signal(barrier, inc=1, device_id=peer, device_id_type=MESH)
    pl.semaphore_wait(barrier, len(peers))

    point_copies = []
    for d in range(1, seg_size):
        copy = pltpu.make_async_remote_copy(
            src_ref=points_ref, dst_ref=peer_points.at[d - 1],
            send_sem=point_send.at[d - 1], recv_sem=point_recv.at[d - 1],
            device_id=seg_peer(d), device_id_type=MESH)
        copy.start()
        point_copies.append(copy)

    def absorb(points, first, last):
        x = [points[k:k + 1, :] - centre_ref[k:k + 1, 0:1] for k in range(3)]
        rows = []
        for k in range(3):
            rows += right_rows(x[k])
        rows += right_rows(x[0] * x[0] + x[1] * x[1] + x[2] * x[2])
        rows += [jnp.ones((1, local), f32)] * 3
        rows += [jnp.zeros((1, local), f32)] * (DEPTH - len(rows))
        side[...] = jnp.concatenate(rows, axis=0).astype(bf16)

        def step(i, carry):
            for j in range(GROUP):
                rows = pl.ds(pl.multiple_of(i * (CHUNK * GROUP) + j * CHUNK, CHUNK), CHUNK)
                a2 = jnp.dot(near_ref[rows, :], side[...], preferred_element_type=f32)
                b2 = jnp.dot(far_ref[rows, :], side[...], preferred_element_type=f32)
                ra = lax.rsqrt(a2)
                rb = lax.rsqrt(b2)
                total = a2 * ra + b2 * rb
                factor = (ra + rb) * pl.reciprocal(total * total - 1.0, approx=True)
                hi = factor.astype(bf16)
                hi_buf[j * CHUNK:(j + 1) * CHUNK, :] = hi
                lo_buf[j * CHUNK:(j + 1) * CHUNK, :] = (factor - hi.astype(f32)).astype(bf16)
            cols = pl.ds(pl.multiple_of(i * (CHUNK * GROUP), CHUNK * GROUP), CHUNK * GROUP)
            both_acc[...] += jnp.dot(weight_ref[:, cols], hi_buf[...], preferred_element_type=f32)
            low_acc[...] += jnp.dot(weight_ref[0:6 * SNAPS, cols], lo_buf[...], preferred_element_type=f32)
            return carry

        lax.fori_loop(first, last, step, 0)
        return x

    def clear():
        both_acc[...] = jnp.zeros_like(both_acc)
        low_acc[...] = jnp.zeros_like(low_acc)

    def collect(x):
        g = both_acc[0:6 * SNAPS, :] + both_acc[6 * SNAPS:12 * SNAPS, :] + low_acc[...]
        g = [g[SNAPS * k:SNAPS * (k + 1), :] for k in range(6)]
        return [
            x[1] * g[2] - x[2] * g[1] + g[3],
            x[2] * g[0] - x[0] * g[2] + g[4],
            x[0] * g[1] - x[1] * g[0] + g[5],
        ]

    steps = segs // (CHUNK * GROUP)
    part_copies = []
    for d in range(1, seg_size):
        point_copies[d - 1].wait()
        clear()
        x = absorb(peer_points[d - 1], 0, steps)
        for c, block in enumerate(collect(x)):
            part_out[d - 1, SNAPS * c:SNAPS * (c + 1), :] = block
        copy = pltpu.make_async_remote_copy(
            src_ref=part_out.at[d - 1], dst_ref=part_in.at[d - 1],
            send_sem=part_send.at[d - 1], recv_sem=part_recv.at[d - 1],
            device_id=seg_peer(seg_size - d), device_id_type=MESH)
        copy.start()
        part_copies.append(copy)
    clear()
    x = absorb(points_ref[...], 0, steps)
    panel = jnp.concatenate(collect(x), axis=0)
    for d in range(1, seg_size):
        part_copies[d - 1].wait()
        panel = panel + part_in[d - 1]

    def all_sum(ref, slots, send, recv):
        for k in range(bits):
            copy = pltpu.make_async_remote_copy(
                src_ref=ref, dst_ref=slots.at[k], send_sem=send.at[k], recv_sem=recv.at[k],
                device_id=bit_peer(k), device_id_type=MESH)
            copy.start()
            copy.wait()
            ref[...] += slots[k]

    across = (((1,), (1,)), ((), ()))
    coeff_ref[...] = lax.dot_general(panel, modes_ref[...], across, precision=HIGH, preferred_element_type=f32)
    all_sum(coeff_ref, coeff_in, coeff_send, coeff_recv)
    proj = panel - jnp.dot(coeff_ref[...], modes_ref[...], precision=HIGH, preferred_element_type=f32)
    proj_ref[...] = proj
    gram_ref[...] = lax.dot_general(proj, proj, across, precision=HIGH, preferred_element_type=f32) * (
        1.0 / (count * local))
    all_sum(gram_ref, gram_in, gram_send, gram_recv)


def solve_kernel(gram_ref, proj_ref, factor_ref, basis_ref):
    order = gram_ref.shape[0]
    tiles = order // 8
    gram = [gram_ref[8 * t:8 * t + 8, :] for t in range(tiles)]
    right = [proj_ref[8 * t:8 * t + 8, :] for t in range(tiles)]
    row = lax.broadcasted_iota(jnp.int32, (8, 1), 0)
    for k in range(order):
        at, r = k // 8, k % 8
        line = gram[at][r:r + 1, :]
        inv = lax.rsqrt(line[:, k:k + 1])
        line = line * inv
        side = right[at][r:r + 1, :] * inv
        for t in range(at, tiles):
            col = gram[t][:, k:k + 1] * inv
            if t == at:
                col = jnp.where(row > r, col, 0.0)
            gram[t] = gram[t] - col * line
            right[t] = right[t] - col * side
        gram[at] = jnp.where(row == r, line, gram[at])
        right[at] = jnp.where(row == r, side, right[at])
    col = lax.broadcasted_iota(jnp.int32, (8, order), 1)
    for t in range(tiles):
        factor_ref[8 * t:8 * t + 8, :] = jnp.where(col >= row + 8 * t, gram[t], 0.0)
        basis_ref[8 * t:8 * t + 8, :] = right[t]


def body(pts_size, seg_size, field_points, wake_nodes, trail_node, strength, core_square, snapshot, stored_modes):
    segs = wake_nodes.shape[1]
    local = field_points.shape[1]
    modes = stored_modes.shape[0]
    rank = 3 * SNAPS
    bits = (pts_size * seg_size).bit_length() - 1
    shape = jax.ShapeDtypeStruct
    vmem = pl.BlockSpec(memory_space=pltpu.VMEM)
    near, far, weight, centre = pl.pallas_call(
        prep_kernel,
        out_shape=(
            shape((segs, DEPTH), bf16), shape((segs, DEPTH), bf16),
            shape((12 * SNAPS, segs), bf16), shape((3, 128), f32)),
        in_specs=[vmem] * 5,
        out_specs=(vmem,) * 4,
        scratch_shapes=[pltpu.VMEM((3, segs), f32)],
        compiler_params=pltpu.CompilerParams(vmem_limit_bytes=40 * 1024 * 1024),
        name="prep",
    )(wake_nodes, trail_node.reshape(segs // 128, 128), strength[None], core_square[None], snapshot[None])
    peers = seg_size - 1
    dma = pltpu.SemaphoreType.DMA
    coeffs, gram, proj = pl.pallas_call(
        functools.partial(main_kernel, pts_size, seg_size),
        out_shape=(shape((rank, modes), f32), shape((rank, rank), f32), shape((rank, local), f32)),
        in_specs=[vmem] * 6,
        out_specs=(vmem,) * 3,
        scratch_shapes=[
            pltpu.VMEM((peers, 3, local), f32),
            pltpu.VMEM((peers, rank, local), f32),
            pltpu.VMEM((peers, rank, local), f32),
            pltpu.VMEM((12 * SNAPS, local), f32),
            pltpu.VMEM((6 * SNAPS, local), f32),
            pltpu.VMEM((DEPTH, local), bf16),
            pltpu.VMEM((CHUNK * GROUP, local), bf16),
            pltpu.VMEM((CHUNK * GROUP, local), bf16),
            pltpu.VMEM((bits, rank, modes), f32),
            pltpu.VMEM((bits, rank, rank), f32),
            dma((peers,)), dma((peers,)), dma((peers,)), dma((peers,)),
            dma((bits,)), dma((bits,)), dma((bits,)), dma((bits,)),
        ],
        compiler_params=pltpu.CompilerParams(
            collective_id=0, has_side_effects=True, vmem_limit_bytes=40 * 1024 * 1024),
        name="main",
    )(field_points, near, far, weight, centre, stored_modes)
    factor, basis = pl.pallas_call(
        solve_kernel,
        out_shape=(shape((rank, rank), f32), shape((rank, local), f32)),
        in_specs=[vmem] * 2,
        out_specs=(vmem,) * 2,
        name="solve",
    )(gram, proj)
    return coeffs.T, factor, basis


def solution(mesh):
    return jax.shard_map(
        functools.partial(body, mesh.shape["pts"], mesh.shape["seg"]),
        mesh=mesh,
        in_specs=(
            P(None, ("groups", "pts", "seg")),
            P(None, ("groups", "seg")),
            P(("groups", "seg")),
            P(("groups", "seg")),
            P(("groups", "seg")),
            P(("groups", "seg")),
            P(None, ("groups", "pts", "seg")),
        ),
        out_specs=(P("groups", None), P("groups", None), P(None, ("groups", "pts", "seg"))),
        check_vma=False,
    )
```

time: 624 us -> 88.8 us (0.14)
  other arithmetic: 289 us -> 0 us
  waiting for transfers between devices: 113 us -> 0 us
  matrix products: 87.6 us -> 0 us
  Pallas kernels: 0 us -> 80 us
  blocking collectives: 58.6 us -> 0 us
  local copies, waits for them, and re-layouts: 59 us -> 7.5 us
  between operations: 14.2 us -> 0.68 us
    reduce_sum x16 -> x0, other arithmetic: 133 us -> none  [induced_block(): near_len = jnp.sqrt(jnp.sum(near_arm * near_arm, axis=0) + core_sq)]
    psum x1 -> x0, waiting for transfers between devices: 87.3 us -> none  [body(): coeffs = lax.psum(matmul(stored_modes, panel.T), ('pts', 'seg'))]
    dot_general x19 -> x0, matrix products: 86.7 us -> none  [the longest x16 84 us: induced_block(): induced = jnp.einsum('cpn,ns->csp', curl_dir, weights, precision=HIGH)]
    pallas_call x0 -> x3, Pallas kernels: none -> 80 us  [the longest x1 62.9 us: body(): pl.pallas_call(functools.partial(main_kernel, pts_size, seg_size), out_sh...]
    sub x16 -> x0, other arithmetic: 68.4 us -> none  [induced_block(): near_arm[1] * far_arm[2] - near_arm[2] * far_arm[1]]
    div x18 -> x0, other arithmetic: 61.9 us -> none  [the longest x16 61.9 us: induced_block(): (near_len + far_len) / (near_len * far_len * (near_len * far_len + along_...]
    psum x1 -> x0, blocking collectives: 58.6 us -> none  [body(): lax.psum(matmul(projected, projected.T), ('pts', 'seg')) / total_points]
    gather x2 -> x0, local copies, waits for them, and re-layouts: 32.8 us -> none  [body(): seg_ends = wake_nodes[:, trail_node]]
  transfers between devices with their start and end apart: 2 -> 0, of which waited for: 2 -> 0; matrix products, arithmetic and copies ran while one was open for 0% -> 0% of each run, Pallas kernels for 0% -> 0%
where the time goes in v1:
time: 88.8 us; the launch traced here: 88.2 us
  Pallas kernels  80 us (90%)
  local copies, waits for them, and re-layouts  7.5 us (8%)
    pallas_call x1, Pallas kernels, body(): pl.pallas_call(functools.partial(main_kernel, pts_size, seg_size), out_sh...  62.9 us
    pallas_call x1, Pallas kernels, body(): pl.pallas_call(prep_kernel, out_shape=(shape((segs, DEPTH), bf16), shape(...  11.7 us
    unnamed x19, local copies, waits for them, and re-layouts  7.5 us
    pallas_call x1, Pallas kernels, body(): pl.pallas_call(solve_kernel, out_shape=(shape((rank, rank), f32), shape((...  5.42 us

profile of v1, /device:TPU:0, one launch (start us, length us, event | category | flops | bytes accessed | tf_op | source)
XLA Modules:
  0.0 88.2 jit_solution(12708870103587026917)
XLA Ops:
  0.6 0.0 copy-start.1
  0.6 0.9 %copy-done.1 = f32[3,8192]{1,0:T(4,128)S(1)} copy-done((f32[3,8192]{1,0:T(4,128)S(1)}, f32[3,8192]{1,0:T(4,128)}, u32[]{:S(2)}) %copy-start.1) | copy-done | bytes 98328
  1.5 0.0 copy-start.3
  1.5 0.8 copy-done.3
  2.3 0.0 copy-start.4
  2.3 0.8 copy-done.4
  3.1 0.0 copy-start.5
  3.1 0.8 copy-done.5
  3.8 0.0 copy-start.6
  3.8 0.8 copy-done.6
  4.6 11.7 %prep.1 = (bf16[8192,32]{1,0:T(8,128)(2,1)S(1)}, bf16[8192,32]{1,0:T(8,128)(2,1)S(1)}, bf16[192,8192]{1,0:T(8,128)(2,1)S(1)}, f32[3,128]{1,0:T(4,128)S(1)}) custom-call(f32[3,8192]{1,0:T(4,128)S(1)} %copy-done.1, s32[64,128]{1,0:T(8,128)S(1)} %bitcast.6, f32[1,8192]{1,0:T(1,128)S(1)} %bitcast.7, f32[1,8192]{1,0:T(1,128)S(1)} %bitcast.8, s32[1,8192]{1,0:T(1,128)S(1)} %bitcast.9), custom_call_target="tpu_custom_call" | custom-call | tf_op jit(solution)/shard_map/prep/pallas_call | solution.py:259
  16.3 0.0 copy-start
  16.3 1.0 %copy-done = f32[512,256]{1,0:T(8,128)S(1)} copy-done((f32[512,256]{1,0:T(8,128)S(1)}, f32[512,256]{1,0:T(8,128)}, u32[]{:S(2)}) %copy-start) | copy-done | bytes 524312
  17.3 0.0 copy-start.8
  17.3 0.7 copy-done.8
  18.0 62.9 %main.1 = (f32[48,512]{1,0:T(8,128)S(1)}, f32[48,48]{1,0:T(8,128)S(1)}, f32[48,256]{1,0:T(8,128)S(1)}) custom-call(f32[3,256]{1,0:T(4,128)S(1)} %copy-done.8, bf16[8192,32]{1,0:T(8,128)(2,1)S(1)} %get-tuple-element.12.near_ref, bf16[8192,32]{1,0:T(8,128)(2,1)S(1)} %get-tuple-element.13.far_ref, bf16[192,8192]{1,0:T(8,128)(2,1)S(1)} %get-tuple-element.14.weight_ref, ...), custom_call_target="tpu_custom_call" | custom-call | tf_op jit(solution)/shard_map/main/pallas_call | solution.py:272
  80.9 0.0 copy-start.2
  80.9 0.6 copy-done.2
  81.6 0.0 copy-start.7
  81.6 0.6 copy-done.7
  82.2 5.4 %solve.1 = (f32[48,48]{1,0:T(8,128)}, f32[48,256]{1,0:T(8,128)}) custom-call(f32[48,48]{1,0:T(8,128)} %copy-done.7, f32[48,256]{1,0:T(8,128)} %copy-done.2), custom_call_target="tpu_custom_call" | custom-call | tf_op jit(solution)/shard_map/solve/pallas_call | solution.py:295
  87.6 0.6 copy.11
Async XLA Ops:
  0.6 0.9 %copy-start.1 = (f32[3,8192]{1,0:T(4,128)S(1)}, f32[3,8192]{1,0:T(4,128)}, u32[]{:S(2)}) copy-start(f32[3,8192]{1,0:T(4,128)} %nodes_ref.1) | copy-start | bytes 294916
  1.5 0.8 copy-start.3
  2.3 0.8 copy-start.4
  3.1 0.8 copy-start.5
  3.8 0.8 copy-start.6
  16.3 1.0 %copy-start = (f32[512,256]{1,0:T(8,128)S(1)}, f32[512,256]{1,0:T(8,128)}, u32[]{:S(2)}) copy-start(f32[512,256]{1,0:T(8,128)} %modes_ref.1) | copy-start | bytes 1572868
  17.3 0.7 copy-start.8
  80.9 0.6 copy-start.2
  81.6 0.6 copy-start.7

commit v2 on v1

--- a/solution.py
+++ b/solution.py
@@ -13,7 +13,7 @@
 MESH = pl.DeviceIdType.MESH
 DEPTH = 32
 CHUNK = 256
-GROUP = 4
+GROUP = 8
 f32 = jnp.float32
 bf16 = jnp.bfloat16
 
@@ -35,8 +35,16 @@
     return [hi, mid, hi, lo, hi, mid]
 
 
-def prep_kernel(nodes_ref, trail_ref, strength_ref, core_ref, snap_ref,
-                near_ref, far_ref, weight_ref, centre_ref, head_ref):
+def prep_kernel(nodes_in, trail_in, strength_in, core_in, snap_in,
+                near_ref, far_ref, weight_ref, centre_ref,
+                nodes_ref, trail_ref, strength_ref, core_ref, snap_ref, head_ref, sems):
+    pairs = ((nodes_in, nodes_ref), (trail_in, trail_ref), (strength_in, strength_ref),
+             (core_in, core_ref), (snap_in, snap_ref))
+    copies = [pltpu.make_async_copy(a, b, sems.at[i]) for i, (a, b) in enumerate(pairs)]
+    for copy in copies:
+        copy.start()
+    copies[0].wait()
+    copies[1].wait()
     segs = nodes_ref.shape[1]
     rows = segs // 128
     nodes = nodes_ref[...]
@@ -65,6 +73,8 @@
                 at = (8 * r + i) * 128
                 head_ref[k:k + 1, at:at + 128] = found[3 * r + k][i:i + 1, :]
 
+    for copy in copies[2:]:
+        copy.wait()
     width = 1024
     zero = jnp.zeros((1, width), f32)
     levels = lax.broadcasted_iota(jnp.int32, (SNAPS, width), 0)
@@ -101,46 +111,45 @@
     lax.fori_loop(0, segs // width, fill, 0)
 
 
-def main_kernel(pts_size, seg_size, points_ref, near_ref, far_ref, weight_ref, centre_ref, modes_ref,
+def main_kernel(pts_size, seg_size, points_ref, near_ref, far_ref, weight_ref, centre_ref, modes_in,
                 coeff_ref, gram_ref, proj_ref,
-                peer_points, part_out, part_in, both_acc, low_acc, side, hi_buf, lo_buf,
-                coeff_in, gram_in,
-                point_send, point_recv, part_send, part_recv, coeff_send, coeff_recv, gram_send, gram_recv):
+                points, modes_ref, peer_points, part_out, part_in, own_both, own_low, both_acc, low_acc,
+                side, hi_buf, lo_buf, coeff_part, coeff_seg, coeff_pts, coeff_mine, coeff_all, gram_part, gram_seg, gram_pts,
+                local_sem, point_send, point_recv, part_send, part_recv,
+                send_a, recv_a, send_b, recv_b, send_c, recv_c, send_d, recv_d, send_e, recv_e):
     group = lax.axis_index("groups")
     pts = lax.axis_index("pts")
     seg = lax.axis_index("seg")
-    count = pts_size * seg_size
-    bits = count.bit_length() - 1
-    flat = pts * seg_size + seg
     segs = near_ref.shape[0]
     local = points_ref.shape[1]
+    rank = 3 * SNAPS
+    width = modes_in.shape[0] // seg_size
 
     def seg_peer(d):
         return (group, pts, lax.rem(seg + d, seg_size))
 
-    def bit_peer(k):
-        bit = 1 << k
-        other = flat + (1 - 2 * ((flat // bit) % 2)) * bit
-        return (group, other // seg_size, other % seg_size)
-
-    peers = [seg_peer(d) for d in range(1, seg_size)]
-    peers += [bit_peer(k) for k in range(bits)]
+    def pts_peer(d):
+        return (group, lax.rem(pts + d, pts_size), seg)
+
     barrier = pltpu.get_barrier_semaphore()
+    peers = [seg_peer(d) for d in range(1, seg_size)] + [pts_peer(d) for d in range(1, pts_size)]
     for peer in peers:
         pl.semaphore_signal(barrier, inc=1, device_id=peer, device_id_type=MESH)
-    pl.semaphore_wait(barrier, len(peers))
-
-    point_copies = []
-    for d in range(1, seg_size):
+
+    get_points = pltpu.make_async_copy(points_ref, points, local_sem.at[0])
+    get_points.start()
+    get_modes = pltpu.make_async_copy(modes_in, modes_ref, local_sem.at[1])
+    get_modes.start()
+
+    def send(src, dst, send_sem, recv_sem, peer):
         copy = pltpu.make_async_remote_copy(
-            src_ref=points_ref, dst_ref=peer_points.at[d - 1],
-            send_sem=point_send.at[d - 1], recv_sem=point_recv.at[d - 1],
-            device_id=seg_peer(d), device_id_type=MESH)
+            src_ref=src, dst_ref=dst, send_sem=send_sem, recv_sem=recv_sem,
+            device_id=peer, device_id_type=MESH)
         copy.start()
-        point_copies.append(copy)
-
-    def absorb(points, first, last):
-        x = [points[k:k + 1, :] - centre_ref[k:k + 1, 0:1] for k in range(3)]
+        return copy
+
+    def place(raw):
+        x = [raw[k:k + 1, :] - centre_ref[k:k + 1, 0:1] for k in range(3)]
         rows = []
         for k in range(3):
             rows += right_rows(x[k])
@@ -148,7 +157,9 @@
         rows += [jnp.ones((1, local), f32)] * 3
         rows += [jnp.zeros((1, local), f32)] * (DEPTH - len(rows))
         side[...] = jnp.concatenate(rows, axis=0).astype(bf16)
-
+        return x
+
+    def absorb(both, low, first, last):
         def step(i, carry):
             for j in range(GROUP):
                 rows = pl.ds(pl.multiple_of(i * (CHUNK * GROUP) + j * CHUNK, CHUNK), CHUNK)
@@ -162,19 +173,14 @@
                 hi_buf[j * CHUNK:(j + 1) * CHUNK, :] = hi
                 lo_buf[j * CHUNK:(j + 1) * CHUNK, :] = (factor - hi.astype(f32)).astype(bf16)
             cols = pl.ds(pl.multiple_of(i * (CHUNK * GROUP), CHUNK * GROUP), CHUNK * GROUP)
-            both_acc[...] += jnp.dot(weight_ref[:, cols], hi_buf[...], preferred_element_type=f32)
-            low_acc[...] += jnp.dot(weight_ref[0:6 * SNAPS, cols], lo_buf[...], preferred_element_type=f32)
+            both[...] += jnp.dot(weight_ref[:, cols], hi_buf[...], preferred_element_type=f32)
+            low[...] += jnp.dot(weight_ref[0:6 * SNAPS, cols], lo_buf[...], preferred_element_type=f32)
             return carry
 
         lax.fori_loop(first, last, step, 0)
-        return x
-
-    def clear():
-        both_acc[...] = jnp.zeros_like(both_acc)
-        low_acc[...] = jnp.zeros_like(low_acc)
-
-    def collect(x):
-        g = both_acc[0:6 * SNAPS, :] + both_acc[6 * SNAPS:12 * SNAPS, :] + low_acc[...]
+
+    def collect(x, both, low):
+        g = both[0:6 * SNAPS, :] + both[6 * SNAPS:12 * SNAPS, :] + low[...]
         g = [g[SNAPS * k:SNAPS * (k + 1), :] for k in range(6)]
         return [
             x[1] * g[2] - x[2] * g[1] + g[3],
@@ -183,43 +189,78 @@
         ]
 
     steps = segs // (CHUNK * GROUP)
+    cut = (steps // 4, steps - steps // 4)
+    own_both[...] = jnp.zeros_like(own_both)
+    own_low[...] = jnp.zeros_like(own_low)
+    get_points.wait()
+    place(points[...])
+    absorb(own_both, own_low, 0, cut[0])
+    pl.semaphore_wait(barrier, len(peers))
+    point_copies = [
+        send(points, peer_points.at[d - 1], point_send.at[d - 1], point_recv.at[d - 1], seg_peer(d))
+        for d in range(1, seg_size)]
+    absorb(own_both, own_low, cut[0], cut[1])
+
     part_copies = []
     for d in range(1, seg_size):
         point_copies[d - 1].wait()
-        clear()
-        x = absorb(peer_points[d - 1], 0, steps)
-        for c, block in enumerate(collect(x)):
+        both_acc[...] = jnp.zeros_like(both_acc)
+        low_acc[...] = jnp.zeros_like(low_acc)
+        x = place(peer_points[d - 1])
+        absorb(both_acc, low_acc, 0, steps)
+        for c, block in enumerate(collect(x, both_acc, low_acc)):
             part_out[d - 1, SNAPS * c:SNAPS * (c + 1), :] = block
-        copy = pltpu.make_async_remote_copy(
-            src_ref=part_out.at[d - 1], dst_ref=part_in.at[d - 1],
-            send_sem=part_send.at[d - 1], recv_sem=part_recv.at[d - 1],
-            device_id=seg_peer(seg_size - d), device_id_type=MESH)
-        copy.start()
-        part_copies.append(copy)
-    clear()
-    x = absorb(points_ref[...], 0, steps)
-    panel = jnp.concatenate(collect(x), axis=0)
+        part_copies.append(send(
+            part_out.at[d - 1], part_in.at[d - 1], part_send.at[d - 1], part_recv.at[d - 1],
+            seg_peer(seg_size - d)))
+    x = place(points[...])
+    absorb(own_both, own_low, cut[1], steps)
+    panel = jnp.concatenate(collect(x, own_both, own_low), axis=0)
     for d in range(1, seg_size):
         part_copies[d - 1].wait()
         panel = panel + part_in[d - 1]
-
-    def all_sum(ref, slots, send, recv):
-        for k in range(bits):
-            copy = pltpu.make_async_remote_copy(
-                src_ref=ref, dst_ref=slots.at[k], send_sem=send.at[k], recv_sem=recv.at[k],
-                device_id=bit_peer(k), device_id_type=MESH)
-            copy.start()
+    get_modes.wait()
+
+    def spread(src_of, dst, mine, size, peer_of, send_sem, recv_sem):
+        copies = [
+            send(src_of(d), dst.at[mine], send_sem.at[d - 1], recv_sem.at[d - 1], peer_of(d))
+            for d in range(1, size)]
+        for copy in copies:
             copy.wait()
-            ref[...] += slots[k]
+
+    def added(slots, size):
+        total = slots[0]
+        for i in range(1, size):
+            total = total + slots[i]
+        return total
 
     across = (((1,), (1,)), ((), ()))
-    coeff_ref[...] = lax.dot_general(panel, modes_ref[...], across, precision=HIGH, preferred_element_type=f32)
-    all_sum(coeff_ref, coeff_in, coeff_send, coeff_recv)
-    proj = panel - jnp.dot(coeff_ref[...], modes_ref[...], precision=HIGH, preferred_element_type=f32)
+    for q in range(seg_size):
+        coeff_part[q] = lax.dot_general(
+            panel, modes_ref[q * width:(q + 1) * width, :], across, precision=HIGH, preferred_element_type=f32)
+    coeff_seg[seg] = coeff_part[seg]
+    spread(lambda d: coeff_part.at[lax.rem(seg + d, seg_size)], coeff_seg, seg, seg_size, seg_peer, send_a, recv_a)
+    coeff_mine[0] = added(coeff_seg, seg_size)
+    coeff_pts[pts] = coeff_mine[0]
+    spread(lambda d: coeff_mine.at[0], coeff_pts, pts, pts_size, pts_peer, send_b, recv_b)
+    coeff_mine[1] = added(coeff_pts, pts_size)
+    coeff_all[seg] = coeff_mine[1]
+    spread(lambda d: coeff_mine.at[1], coeff_all, seg, seg_size, seg_peer, send_c, recv_c)
+    proj = panel
+    for q in range(seg_size):
+        block = coeff_all[q]
+        coeff_ref[:, q * width:(q + 1) * width] = block
+        proj = proj - jnp.dot(
+            block, modes_ref[q * width:(q + 1) * width, :], precision=HIGH, preferred_element_type=f32)
     proj_ref[...] = proj
-    gram_ref[...] = lax.dot_general(proj, proj, across, precision=HIGH, preferred_element_type=f32) * (
-        1.0 / (count * local))
-    all_sum(gram_ref, gram_in, gram_send, gram_recv)
+    gram_part[0] = lax.dot_general(proj, proj, across, precision=HIGH, preferred_element_type=f32) * (
+        1.0 / (pts_size * seg_size * local))
+    gram_seg[seg] = gram_part[0]
+    spread(lambda d: gram_part.at[0], gram_seg, seg, seg_size, seg_peer, send_d, recv_d)
+    gram_part[1] = added(gram_seg, seg_size)
+    gram_pts[pts] = gram_part[1]
+    spread(lambda d: gram_part.at[1], gram_pts, pts, pts_size, pts_peer, send_e, recv_e)
+    gram_ref[...] = added(gram_pts, pts_size)
 
 
 def solve_kernel(gram_ref, proj_ref, factor_ref, basis_ref):
@@ -253,43 +294,60 @@
     local = field_points.shape[1]
     modes = stored_modes.shape[0]
     rank = 3 * SNAPS
-    bits = (pts_size * seg_size).bit_length() - 1
     shape = jax.ShapeDtypeStruct
     vmem = pl.BlockSpec(memory_space=pltpu.VMEM)
+    hbm = pl.BlockSpec(memory_space=pl.ANY)
+    dma = pltpu.SemaphoreType.DMA
     near, far, weight, centre = pl.pallas_call(
         prep_kernel,
         out_shape=(
             shape((segs, DEPTH), bf16), shape((segs, DEPTH), bf16),
             shape((12 * SNAPS, segs), bf16), shape((3, 128), f32)),
-        in_specs=[vmem] * 5,
+        in_specs=[hbm] * 5,
         out_specs=(vmem,) * 4,
-        scratch_shapes=[pltpu.VMEM((3, segs), f32)],
-        compiler_params=pltpu.CompilerParams(vmem_limit_bytes=40 * 1024 * 1024),
+        scratch_shapes=[
+            pltpu.VMEM((3, segs), f32), pltpu.VMEM((segs // 128, 128), jnp.int32),
+            pltpu.VMEM((1, segs), f32), pltpu.VMEM((1, segs), f32), pltpu.VMEM((1, segs), jnp.int32),
+            pltpu.VMEM((3, segs), f32), dma((5,))],
+        compiler_params=pltpu.CompilerParams(vmem_limit_bytes=50 * 1024 * 1024),
         name="prep",
     )(wake_nodes, trail_node.reshape(segs // 128, 128), strength[None], core_square[None], snapshot[None])
     peers = seg_size - 1
-    dma = pltpu.SemaphoreType.DMA
+    far_peers = pts_size - 1
+    width = modes // seg_size
     coeffs, gram, proj = pl.pallas_call(
         functools.partial(main_kernel, pts_size, seg_size),
         out_shape=(shape((rank, modes), f32), shape((rank, rank), f32), shape((rank, local), f32)),
-        in_specs=[vmem] * 6,
+        in_specs=[hbm] + [vmem] * 4 + [hbm],
         out_specs=(vmem,) * 3,
         scratch_shapes=[
+            pltpu.VMEM((3, local), f32),
+            pltpu.VMEM((modes, local), f32),
             pltpu.VMEM((peers, 3, local), f32),
             pltpu.VMEM((peers, rank, local), f32),
             pltpu.VMEM((peers, rank, local), f32),
             pltpu.VMEM((12 * SNAPS, local), f32),
             pltpu.VMEM((6 * SNAPS, local), f32),
+            pltpu.VMEM((12 * SNAPS, local), f32),
+            pltpu.VMEM((6 * SNAPS, local), f32),
             pltpu.VMEM((DEPTH, local), bf16),
             pltpu.VMEM((CHUNK * GROUP, local), bf16),
             pltpu.VMEM((CHUNK * GROUP, local), bf16),
-            pltpu.VMEM((bits, rank, modes), f32),
-            pltpu.VMEM((bits, rank, rank), f32),
+            pltpu.VMEM((seg_size, rank, width), f32),
+            pltpu.VMEM((seg_size, rank, width), f32),
+            pltpu.VMEM((pts_size, rank, width), f32),
+            pltpu.VMEM((2, rank, width), f32),
+            pltpu.VMEM((seg_size, rank, width), f32),
+            pltpu.VMEM((2, rank, rank), f32),
+            pltpu.VMEM((seg_size, rank, rank), f32),
+            pltpu.VMEM((pts_size, rank, rank), f32),
+            dma((2,)),
             dma((peers,)), dma((peers,)), dma((peers,)), dma((peers,)),
-            dma((bits,)), dma((bits,)), dma((bits,)), dma((bits,)),
+            dma((peers,)), dma((peers,)), dma((far_peers,)), dma((far_peers,)), dma((peers,)), dma((peers,)),
+            dma((peers,)), dma((peers,)), dma((far_peers,)), dma((far_peers,)),
         ],
         compiler_params=pltpu.CompilerParams(
-            collective_id=0, has_side_effects=True, vmem_limit_bytes=40 * 1024 * 1024),
+            collective_id=0, has_side_effects=True, vmem_limit_bytes=50 * 1024 * 1024),
         name="main",
     )(field_points, near, far, weight, centre, stored_modes)
     factor, basis = pl.pallas_call(

time: 88.8 us -> 78.4 us (0.88)
  Pallas kernels: 80 us -> 69.6 us
    pallas_call x1, Pallas kernels: 62.9 us -> 50.2 us  [body(): pl.pallas_call(functools.partial(main_kernel, pts_size, seg_size), out_sh...]
    pallas_call x1, Pallas kernels: 11.7 us -> 14 us  [body(): pl.pallas_call(prep_kernel, out_shape=(shape((segs, DEPTH), bf16), shape(...]
where the time goes in v2:
time: 78.4 us; the launch traced here: 77.8 us
  Pallas kernels  69.6 us (89%)
  local copies, waits for them, and re-layouts  7.5 us (10%)
    pallas_call x1, Pallas kernels, body(): pl.pallas_call(functools.partial(main_kernel, pts_size, seg_size), out_sh...  50.2 us
    pallas_call x1, Pallas kernels, body(): pl.pallas_call(prep_kernel, out_shape=(shape((segs, DEPTH), bf16), shape(...  14 us
    unnamed x19, local copies, waits for them, and re-layouts  7.5 us
    pallas_call x1, Pallas kernels, body(): pl.pallas_call(solve_kernel, out_shape=(shape((rank, rank), f32), shape((...  5.42 us

profile of v2, /device:TPU:0, one launch (start us, length us, event | category | flops | bytes accessed | tf_op | source)
XLA Modules:
  0.0 77.8 jit_solution(3519471656437041158)
XLA Ops:
  0.6 0.0 copy-start.1
  0.6 0.9 %copy-done.1 = f32[3,8192]{1,0:T(4,128)S(1)} copy-done((f32[3,8192]{1,0:T(4,128)S(1)}, f32[3,8192]{1,0:T(4,128)}, u32[]{:S(2)}) %copy-start.1) | copy-done | bytes 98328
  1.5 0.0 copy-start.3
  1.5 0.8 copy-done.3
  2.3 0.0 copy-start.4
  2.3 0.8 copy-done.4
  3.1 0.0 copy-start.5
  3.1 0.8 copy-done.5
  3.8 0.0 copy-start.6
  3.8 0.8 copy-done.6
  4.6 14.0 %prep.1 = (bf16[8192,32]{1,0:T(8,128)(2,1)S(1)}, bf16[8192,32]{1,0:T(8,128)(2,1)}, bf16[192,8192]{1,0:T(8,128)(2,1)}, f32[3,128]{1,0:T(4,128)S(1)}) custom-call(f32[3,8192]{1,0:T(4,128)S(1)} %copy-done.1, s32[64,128]{1,0:T(8,128)S(1)} %bitcast.6, f32[1,8192]{1,0:T(1,128)S(1)} %bitcast.7, f32[1,8192]{1,0:T(1,128)S(1)} %bitcast.8, s32[1,8192]{1,0:T(1,128)S(1)} %bitcast.9), custom_call_target="tpu_custom_call" | custom-call | tf_op jit(solution)/shard_map/prep/pallas_call | solution.py:301
  18.6 0.0 copy-start
  18.6 1.0 %copy-done = f32[512,256]{1,0:T(8,128)S(1)} copy-done((f32[512,256]{1,0:T(8,128)S(1)}, f32[512,256]{1,0:T(8,128)}, u32[]{:S(2)}) %copy-start) | copy-done | bytes 524312
  19.6 0.0 copy-start.8
  19.6 0.7 copy-done.8
  20.3 50.2 %main.1 = (f32[48,512]{1,0:T(8,128)S(1)}, f32[48,48]{1,0:T(8,128)S(1)}, f32[48,256]{1,0:T(8,128)S(1)}) custom-call(f32[3,256]{1,0:T(4,128)S(1)} %copy-done.8, bf16[8192,32]{1,0:T(8,128)(2,1)S(1)} %get-tuple-element.12.near_ref, bf16[8192,32]{1,0:T(8,128)(2,1)} %get-tuple-element.13.far_ref, bf16[192,8192]{1,0:T(8,128)(2,1)} %get-tuple-element.14.weight_ref, ...), custom_call_target="tpu_custom_call" | custom-call | tf_op jit(solution)/shard_map/main/pallas_call | solution.py:318
  70.5 0.0 copy-start.2
  70.5 0.6 copy-done.2
  71.2 0.0 copy-start.7
  71.2 0.6 copy-done.7
  71.8 5.4 %solve.1 = (f32[48,48]{1,0:T(8,128)}, f32[48,256]{1,0:T(8,128)}) custom-call(f32[48,48]{1,0:T(8,128)} %copy-done.7, f32[48,256]{1,0:T(8,128)} %copy-done.2), custom_call_target="tpu_custom_call" | custom-call | tf_op jit(solution)/shard_map/solve/pallas_call | solution.py:353
  77.2 0.6 copy.11
Async XLA Ops:
  0.6 0.9 %copy-start.1 = (f32[3,8192]{1,0:T(4,128)S(1)}, f32[3,8192]{1,0:T(4,128)}, u32[]{:S(2)}) copy-start(f32[3,8192]{1,0:T(4,128)} %nodes_in.1) | copy-start | bytes 294916
  1.5 0.8 copy-start.3
  2.3 0.8 copy-start.4
  3.1 0.8 copy-start.5
  3.8 0.8 copy-start.6
  18.6 1.0 %copy-start = (f32[512,256]{1,0:T(8,128)S(1)}, f32[512,256]{1,0:T(8,128)}, u32[]{:S(2)}) copy-start(f32[512,256]{1,0:T(8,128)} %modes_in.1) | copy-start | bytes 1572868
  19.6 0.7 copy-start.8
  70.5 0.6 copy-start.2
  71.2 0.6 copy-start.7

commit v3 on v2

--- a/solution.py
+++ b/solution.py
@@ -35,7 +35,7 @@
     return [hi, mid, hi, lo, hi, mid]
 
 
-def prep_kernel(nodes_in, trail_in, strength_in, core_in, snap_in,
+def prepare(nodes_in, trail_in, strength_in, core_in, snap_in,
                 near_ref, far_ref, weight_ref, centre_ref,
                 nodes_ref, trail_ref, strength_ref, core_ref, snap_ref, head_ref, sems):
     pairs = ((nodes_in, nodes_ref), (trail_in, trail_ref), (strength_in, strength_ref),
@@ -111,8 +111,10 @@
     lax.fori_loop(0, segs // width, fill, 0)
 
 
-def main_kernel(pts_size, seg_size, points_ref, near_ref, far_ref, weight_ref, centre_ref, modes_in,
+def main_kernel(pts_size, seg_size, points_ref, nodes_in, trail_in, strength_in, core_in, snap_in, modes_in,
                 coeff_ref, gram_ref, proj_ref,
+                near_ref, far_ref, weight_ref, centre_ref,
+                nodes_ref, trail_ref, strength_ref, core_ref, snap_ref, head_ref, prep_sems,
                 points, modes_ref, peer_points, part_out, part_in, own_both, own_low, both_acc, low_acc,
                 side, hi_buf, lo_buf, coeff_part, coeff_seg, coeff_pts, coeff_mine, coeff_all, gram_part, gram_seg, gram_pts,
                 local_sem, point_send, point_recv, part_send, part_recv,
@@ -140,6 +142,8 @@
     get_points.start()
     get_modes = pltpu.make_async_copy(modes_in, modes_ref, local_sem.at[1])
     get_modes.start()
+    prepare(nodes_in, trail_in, strength_in, core_in, snap_in, near_ref, far_ref, weight_ref, centre_ref,
+            nodes_ref, trail_ref, strength_ref, core_ref, snap_ref, head_ref, prep_sems)
 
     def send(src, dst, send_sem, recv_sem, peer):
         copy = pltpu.make_async_remote_copy(
@@ -269,20 +273,24 @@
     gram = [gram_ref[8 * t:8 * t + 8, :] for t in range(tiles)]
     right = [proj_ref[8 * t:8 * t + 8, :] for t in range(tiles)]
     row = lax.broadcasted_iota(jnp.int32, (8, 1), 0)
+    width = proj_ref.shape[1]
+    lanes = min(width, 128)
     for k in range(order):
         at, r = k // 8, k % 8
+        cols = [None] * at + [jnp.broadcast_to(gram[t][:, k:k + 1], (8, lanes)) for t in range(at, tiles)]
+        pivot = cols[at][r:r + 1, :]
+        inv = 1.0 / pivot
+        root = lax.rsqrt(pivot)
         line = gram[at][r:r + 1, :]
-        inv = lax.rsqrt(line[:, k:k + 1])
-        line = line * inv
-        side = right[at][r:r + 1, :] * inv
+        side = right[at][r:r + 1, :]
+        step = line * inv[:, :order]
+        push = side * jnp.concatenate([inv] * (width // lanes), axis=1)
+        cols[at] = jnp.where(row > r, cols[at], 0.0)
         for t in range(at, tiles):
-            col = gram[t][:, k:k + 1] * inv
-            if t == at:
-                col = jnp.where(row > r, col, 0.0)
-            gram[t] = gram[t] - col * line
-            right[t] = right[t] - col * side
-        gram[at] = jnp.where(row == r, line, gram[at])
-        right[at] = jnp.where(row == r, side, right[at])
+            gram[t] = gram[t] - cols[t][:, :order] * step
+            right[t] = right[t] - jnp.concatenate([cols[t]] * (width // lanes), axis=1) * push
+        gram[at] = jnp.where(row == r, line * root[:, :order], gram[at])
+        right[at] = jnp.where(row == r, side * jnp.concatenate([root] * (width // lanes), axis=1), right[at])
     col = lax.broadcasted_iota(jnp.int32, (8, order), 1)
     for t in range(tiles):
         factor_ref[8 * t:8 * t + 8, :] = jnp.where(col >= row + 8 * t, gram[t], 0.0)
@@ -298,29 +306,20 @@
     vmem = pl.BlockSpec(memory_space=pltpu.VMEM)
     hbm = pl.BlockSpec(memory_space=pl.ANY)
     dma = pltpu.SemaphoreType.DMA
-    near, far, weight, centre = pl.pallas_call(
-        prep_kernel,
-        out_shape=(
-            shape((segs, DEPTH), bf16), shape((segs, DEPTH), bf16),
-            shape((12 * SNAPS, segs), bf16), shape((3, 128), f32)),
-        in_specs=[hbm] * 5,
-        out_specs=(vmem,) * 4,
-        scratch_shapes=[
-            pltpu.VMEM((3, segs), f32), pltpu.VMEM((segs // 128, 128), jnp.int32),
-            pltpu.VMEM((1, segs), f32), pltpu.VMEM((1, segs), f32), pltpu.VMEM((1, segs), jnp.int32),
-            pltpu.VMEM((3, segs), f32), dma((5,))],
-        compiler_params=pltpu.CompilerParams(vmem_limit_bytes=50 * 1024 * 1024),
-        name="prep",
-    )(wake_nodes, trail_node.reshape(segs // 128, 128), strength[None], core_square[None], snapshot[None])
     peers = seg_size - 1
     far_peers = pts_size - 1
     width = modes // seg_size
     coeffs, gram, proj = pl.pallas_call(
         functools.partial(main_kernel, pts_size, seg_size),
         out_shape=(shape((rank, modes), f32), shape((rank, rank), f32), shape((rank, local), f32)),
-        in_specs=[hbm] + [vmem] * 4 + [hbm],
+        in_specs=[hbm] * 7,
         out_specs=(vmem,) * 3,
         scratch_shapes=[
+            pltpu.VMEM((segs, DEPTH), bf16), pltpu.VMEM((segs, DEPTH), bf16),
+            pltpu.VMEM((12 * SNAPS, segs), bf16), pltpu.VMEM((3, 128), f32),
+            pltpu.VMEM((3, segs), f32), pltpu.VMEM((segs // 128, 128), jnp.int32),
+            pltpu.VMEM((1, segs), f32), pltpu.VMEM((1, segs), f32), pltpu.VMEM((1, segs), jnp.int32),
+            pltpu.VMEM((3, segs), f32), dma((5,)),
             pltpu.VMEM((3, local), f32),
             pltpu.VMEM((modes, local), f32),
             pltpu.VMEM((peers, 3, local), f32),
@@ -347,14 +346,16 @@
             dma((peers,)), dma((peers,)), dma((far_peers,)), dma((far_peers,)),
         ],
         compiler_params=pltpu.CompilerParams(
-            collective_id=0, has_side_effects=True, vmem_limit_bytes=50 * 1024 * 1024),
+            collective_id=0, has_side_effects=True, vmem_limit_bytes=62 * 1024 * 1024),
         name="main",
-    )(field_points, near, far, weight, centre, stored_modes)
+    )(field_points, wake_nodes, trail_node.reshape(segs // 128, 128), strength[None], core_square[None],
+      snapshot[None], stored_modes)
     factor, basis = pl.pallas_call(
         solve_kernel,
         out_shape=(shape((rank, rank), f32), shape((rank, local), f32)),
         in_specs=[vmem] * 2,
         out_specs=(vmem,) * 2,
+        compiler_params=pltpu.CompilerParams(vmem_limit_bytes=62 * 1024 * 1024),
         name="solve",
     )(gram, proj)
     return coeffs.T, factor, basis

time: 78.4 us -> 68 us (0.87)
  local copies, waits for them, and re-layouts: 7.5 us -> 1.54 us
  Pallas kernels: 69.6 us -> 65.6 us
    pallas_call x1 -> x0, Pallas kernels: 14 us -> none  [body(): pl.pallas_call(prep_kernel, out_shape=(shape((segs, DEPTH), bf16), shape(...]
    pallas_call x1, Pallas kernels: 50.2 us -> 60.2 us  [body(): pl.pallas_call(functools.partial(main_kernel, pts_size, seg_size), out_sh...]
    unnamed x19 -> x1, local copies, waits for them, and re-layouts: 7.5 us -> 1.54 us
where the time goes in v3:
time: 68 us; the launch traced here: 67.8 us
  Pallas kernels  65.6 us (96%)
  local copies, waits for them, and re-layouts  1.54 us (2%)
    pallas_call x1, Pallas kernels, body(): pl.pallas_call(functools.partial(main_kernel, pts_size, seg_size), out_sh...  60.2 us
    pallas_call x1, Pallas kernels, body(): pl.pallas_call(solve_kernel, out_shape=(shape((rank, rank), f32), shape((...  5.44 us
    unnamed x1, local copies, waits for them, and re-layouts  1.54 us

profile of v3, /device:TPU:0, one launch (start us, length us, event | category | flops | bytes accessed | tf_op | source)
XLA Modules:
  0.0 67.8 jit_solution(12053602623652320562)
XLA Ops:
  0.6 60.2 %main.1 = (f32[48,512]{1,0:T(8,128)}, f32[48,48]{1,0:T(8,128)}, f32[48,256]{1,0:T(8,128)}) custom-call(f32[3,256]{1,0:T(4,128)} %points_ref.1, f32[3,8192]{1,0:T(4,128)} %nodes_in.1, s32[64,128]{1,0:T(8,128)} %bitcast.6, f32[1,8192]{1,0:T(1,128)} %bitcast.7, f32[1,8192]{1,0:T(1,128)} %bitcast.8, s32[1,8192]{1,0:T(1,128)} %bitcast.9, f32[512,256]{1,0:T(8,128)} %modes_in.1), custom_call_target="tpu_custom_call" | custom-call | tf_op jit(solution)/shard_map/main/pallas_call | solution.py:312
  60.8 5.4 %solve.1 = (f32[48,48]{1,0:T(8,128)}, f32[48,256]{1,0:T(8,128)}) custom-call(f32[48,48]{1,0:T(8,128)} %get-tuple-element.9.gram_ref, f32[48,256]{1,0:T(8,128)} %get-tuple-element.10.proj_ref), custom_call_target="tpu_custom_call" | custom-call | tf_op jit(solution)/shard_map/solve/pallas_call | solution.py:353
  66.3 1.5 %copy.11 = f32[512,48]{0,1:T(8,128)} copy(f32[512,48]{0,1:T(8,128)} %bitcast.5) | data formatting | bytes 196608

commit v4 on v3

--- a/solution.py
+++ b/solution.py
@@ -55,7 +55,12 @@
     high = [trail_ref[8 * r:8 * r + 8, :] // 128 for r in range(tiles)]
     low = [trail_ref[8 * r:8 * r + 8, :] % 128 for r in range(tiles)]
 
-    def look(h, found):
+    def look(block, found):
+        for at in range(8):
+            found = look_row(8 * block + at, found)
+        return found
+
+    def look_row(h, found):
         cols = pl.ds(pl.multiple_of(h * 128, 128), 128)
         out = list(found)
         table = [jnp.broadcast_to(nodes_ref[k:k + 1, cols], (8, 128)) for k in range(3)]
@@ -66,7 +71,7 @@
                 out[3 * r + k] = jnp.where(here, got, out[3 * r + k])
         return tuple(out)
 
-    found = lax.fori_loop(0, rows, look, tuple(jnp.zeros((8, 128), f32) for _ in range(3 * tiles)))
+    found = lax.fori_loop(0, tiles, look, tuple(jnp.zeros((8, 128), f32) for _ in range(3 * tiles)))
     for r in range(tiles):
         for k in range(3):
             for i in range(8):
@@ -239,23 +244,36 @@
         return total
 
     across = (((1,), (1,)), ((), ()))
-    for q in range(seg_size):
-        coeff_part[q] = lax.dot_general(
-            panel, modes_ref[q * width:(q + 1) * width, :], across, precision=HIGH, preferred_element_type=f32)
-    coeff_seg[seg] = coeff_part[seg]
-    spread(lambda d: coeff_part.at[lax.rem(seg + d, seg_size)], coeff_seg, seg, seg_size, seg_peer, send_a, recv_a)
+
+    def modes_of(q):
+        return modes_ref[pl.ds(pl.multiple_of(q * width, width), width), :]
+
+    def product(q):
+        return lax.dot_general(panel, modes_of(q), across, precision=HIGH, preferred_element_type=f32)
+
+    copies = []
+    for d in range(1, seg_size):
+        q = lax.rem(seg + d, seg_size)
+        coeff_part[q] = product(q)
+        copies.append(send(coeff_part.at[q], coeff_seg.at[seg], send_a.at[d - 1], recv_a.at[d - 1], seg_peer(d)))
+    coeff_seg[seg] = product(seg)
+    for copy in copies:
+        copy.wait()
     coeff_mine[0] = added(coeff_seg, seg_size)
     coeff_pts[pts] = coeff_mine[0]
     spread(lambda d: coeff_mine.at[0], coeff_pts, pts, pts_size, pts_peer, send_b, recv_b)
     coeff_mine[1] = added(coeff_pts, pts_size)
     coeff_all[seg] = coeff_mine[1]
-    spread(lambda d: coeff_mine.at[1], coeff_all, seg, seg_size, seg_peer, send_c, recv_c)
-    proj = panel
+    copies = [
+        send(coeff_mine.at[1], coeff_all.at[seg], send_c.at[d - 1], recv_c.at[d - 1], seg_peer(d))
+        for d in range(1, seg_size)]
+    proj = panel - jnp.dot(coeff_mine[1], modes_of(seg), precision=HIGH, preferred_element_type=f32)
+    for d in range(1, seg_size):
+        copies[d - 1].wait()
+        q = lax.rem(seg + seg_size - d, seg_size)
+        proj = proj - jnp.dot(coeff_all[q], modes_of(q), precision=HIGH, preferred_element_type=f32)
     for q in range(seg_size):
-        block = coeff_all[q]
-        coeff_ref[:, q * width:(q + 1) * width] = block
-        proj = proj - jnp.dot(
-            block, modes_ref[q * width:(q + 1) * width, :], precision=HIGH, preferred_element_type=f32)
+        coeff_ref[:, q * width:(q + 1) * width] = coeff_all[q]
     proj_ref[...] = proj
     gram_part[0] = lax.dot_general(proj, proj, across, precision=HIGH, preferred_element_type=f32) * (
         1.0 / (pts_size * seg_size * local))
@@ -267,7 +285,8 @@
     gram_ref[...] = added(gram_pts, pts_size)
 
 
-def solve_kernel(gram_ref, proj_ref, factor_ref, basis_ref):
+def solve_kernel(gram_ref, proj_ref, coeff_ref, factor_ref, basis_ref, coeff_out):
+    coeff_out[...] = coeff_ref[...]
     order = gram_ref.shape[0]
     tiles = order // 8
     gram = [gram_ref[8 * t:8 * t + 8, :] for t in range(tiles)]
@@ -350,14 +369,14 @@
         name="main",
     )(field_points, wake_nodes, trail_node.reshape(segs // 128, 128), strength[None], core_square[None],
       snapshot[None], stored_modes)
-    factor, basis = pl.pallas_call(
+    factor, basis, coeffs = pl.pallas_call(
         solve_kernel,
-        out_shape=(shape((rank, rank), f32), shape((rank, local), f32)),
-        in_specs=[vmem] * 2,
-        out_specs=(vmem,) * 2,
+        out_shape=(shape((rank, rank), f32), shape((rank, local), f32), shape((rank, modes), f32)),
+        in_specs=[vmem] * 3,
+        out_specs=(vmem,) * 3,
         compiler_params=pltpu.CompilerParams(vmem_limit_bytes=62 * 1024 * 1024),
         name="solve",
-    )(gram, proj)
+    )(gram, proj, coeffs)
     return coeffs.T, factor, basis
 
 

time: 68 us -> 62.9 us (0.925)
  Pallas kernels: 65.6 us -> 62.1 us
  local copies, waits for them, and re-layouts: 1.54 us -> 0 us
    pallas_call x1, Pallas kernels: 60.2 us -> 56.5 us  [body(): pl.pallas_call(functools.partial(main_kernel, pts_size, seg_size), out_sh...]
    unnamed x1 -> x0, local copies, waits for them, and re-layouts: 1.54 us -> none
where the time goes in v4:
time: 62.9 us; the launch traced here: 62.7 us
  Pallas kernels  62.1 us (99%)
  between operations  0.64 us (1%)
    pallas_call x1, Pallas kernels, body(): pl.pallas_call(functools.partial(main_kernel, pts_size, seg_size), out_sh...  56.5 us
    pallas_call x1, Pallas kernels, body(): pl.pallas_call(solve_kernel, out_shape=(shape((rank, rank), f32), shape((...  5.6 us

profile of v4, /device:TPU:0, one launch (start us, length us, event | category | flops | bytes accessed | tf_op | source)
XLA Modules:
  0.0 62.7 jit_solution(9583531910902733383)
XLA Ops:
  0.6 56.5 %main.1 = (f32[48,512]{1,0:T(8,128)}, f32[48,48]{1,0:T(8,128)}, f32[48,256]{1,0:T(8,128)}) custom-call(f32[3,256]{1,0:T(4,128)} %points_ref.1, f32[3,8192]{1,0:T(4,128)} %nodes_in.1, s32[64,128]{1,0:T(8,128)} %bitcast.5, f32[1,8192]{1,0:T(1,128)} %bitcast.6, f32[1,8192]{1,0:T(1,128)} %bitcast.7, s32[1,8192]{1,0:T(1,128)} %bitcast.8, f32[512,256]{1,0:T(8,128)} %modes_in.1), custom_call_target="tpu_custom_call" | custom-call | tf_op jit(solution)/shard_map/main/pallas_call | solution.py:331
  57.1 5.6 %solve.1 = (f32[48,48]{1,0:T(8,128)}, f32[48,256]{1,0:T(8,128)}, f32[48,512]{1,0:T(8,128)}) custom-call(f32[48,48]{1,0:T(8,128)} %get-tuple-element.9.gram_ref, f32[48,256]{1,0:T(8,128)} %get-tuple-element.10.proj_ref, f32[48,512]{1,0:T(8,128)} %get-tuple-element.11.coeff_ref), custom_call_target="tpu_custom_call" | custom-call | tf_op jit(solution)/shard_map/solve/pallas_call | solution.py:372
